TPU v7x, 32 devices: a whole 2x2x4 slice. The times are simulated.
32 devices in a mesh: dp: 4 (over y, x), expert: 4 (over z), tensor: 2 (over core).
Axes of the slice: x: 2, y: 2, z: 4, core: 2. Of those that a mesh axis runs over, the one named last changes fastest.
Arguments:
- tokens: bfloat16 [2048, 2048], P(('dp', 'expert')), may hold values from -6 to 6
- expert_ids: int32 [2048, 8], P(('dp', 'expert')), may hold values from 0 to 15, as said below
- gates: float32 [2048, 8], P(('dp', 'expert')), may hold values from 0.05 to 0.5
- token_weight: float32 [2048], P(('dp', 'expert')), may hold values from 0.25 to 4
- w_gate: bfloat16 [16, 2048, 768], P(('dp', 'expert'), None, 'tensor'), may hold values from -0.125 to 0.125
- w_up: bfloat16 [16, 2048, 768], P(('dp', 'expert'), None, 'tensor'), may hold values from -0.125 to 0.125
- w_down: bfloat16 [16, 768, 2048], P(('dp', 'expert'), 'tensor'), may hold values from -0.21875 to 0.21875
- v_gate: bfloat16 [16, 2048, 768], P(('dp', 'expert'), None, 'tensor'), may hold values from -0.125 to 0.125
- v_up: bfloat16 [16, 2048, 768], P(('dp', 'expert'), None, 'tensor'), may hold values from -0.125 to 0.125
- v_down: bfloat16 [16, 768, 2048], P(('dp', 'expert'), 'tensor'), may hold values from -0.21875 to 0.21875
Outputs:
- gv_gate: float32 [16, 2048, 768], P(('dp', 'expert'), None, 'tensor')
- gv_up: float32 [16, 2048, 768], P(('dp', 'expert'), None, 'tensor')
- gv_down: float32 [16, 768, 2048], P(('dp', 'expert'), 'tensor')
- tangent: bfloat16 [2048, 2048], P(('dp', 'expert'), 'tensor')
Inputs may be any that keep to these rules, and one draw needn't show every extreme that they name: `expert_ids`: each row names 8 different experts. Among the 128 rows of one index of dp and expert (aligned blocks of rows) no expert is named more than 128 times, and one expert is named exactly 128 times by the rows of every such block.
All inputs are finite; a program needn't handle non-finite values.
Results may differ from a plain program's by a relative error of at most 0.0063.
Values may be sent and summed in bfloat16 or wider, within the bound.
A program may use at most 256 MiB of HBM per device.

v0:
```python
import functools

import jax
import jax.numpy as jnp
from jax import lax
from jax.experimental import pallas as pl
from jax.experimental.pallas import tpu as pltpu
from jax.sharding import PartitionSpec as P

MESH = pl.DeviceIdType.MESH
ANY = pl.BlockSpec(memory_space=pl.ANY)
AXES = ("dp", "expert")


def product(left, right):
    return jnp.dot(left, right, preferred_element_type=jnp.float32)


def contract_rows(left, right):
    return lax.dot_general(
        left, right, (((0,), (0,)), ((), ())), preferred_element_type=jnp.float32
    )


def silu_parts(pre_gate):
    sigma = jax.nn.sigmoid(pre_gate)
    return (pre_gate * sigma, sigma * (1.0 + pre_gate * (1.0 - sigma)))


def place():
    d, z, c = lax.axis_index("dp"), lax.axis_index("expert"), lax.axis_index("tensor")
    flip_low = d + 1 - 2 * (d % 2)
    flip_high = d + 2 - 4 * (d // 2)
    first = flip_low * (1 - c) + flip_high * c
    second = flip_high * (1 - c) + flip_low * c
    return d, z, c, first, second


def greet(depth):
    d, z, c, first, second = place()
    barrier = pltpu.get_barrier_semaphore()
    peers = [(d, (z + k) % depth, c) for k in range(1, depth)]
    peers += [(first, z, c), (second, z, c), (d, z, 1 - c)]
    for peer in peers:
        pl.semaphore_signal(barrier, inc=1, device_id=peer, device_id_type=MESH)
    pl.semaphore_wait(barrier, len(peers))


def push(src, dst, sems, row, col, peer):
    send, recv = sems
    copy = pltpu.make_async_remote_copy(
        src_ref=src, dst_ref=dst, send_sem=send.at[row, col], recv_sem=recv.at[row, col],
        device_id=peer, device_id_type=MESH,
    )
    copy.start()
    return copy


def spread(depth, src, out, sems, local_sem):
    d, z, c, first, second = place()
    to_first, to_second, to_core = (first, z, c), (second, z, c), (d, z, 1 - c)
    sent, along, one, two, three, cores = [], {}, {}, {}, {}, []
    spot = out.at[d * depth + z, c]
    keep = pltpu.make_async_copy(src, spot, local_sem)
    keep.start()
    for k in range(1, depth):
        along[k] = push(src, spot, sems, 0, k, (d, (z + k) % depth, c))
    for j in range(depth + 1):
        if j < depth:
            from_z = (z - j + depth) % depth
            here = out.at[d * depth + from_z, c]
            if j:
                along[j].wait_recv()
            body = here if j else src
            one[j] = push(body, here, sems, 1, j, to_first)
            two[j] = push(body, here, sems, 2, j, to_second)
            cores.append(push(body, here, sems, 4, j, to_core))
        if j >= 1:
            i = j - 1
            from_z = (z - i + depth) % depth
            one[i].wait_recv()
            here = out.at[first * depth + from_z, c]
            three[i] = push(here, here, sems, 3, i, to_second)
            cores.append(push(here, here, sems, 5, i, to_core))
            two[i].wait_recv()
            here = out.at[second * depth + from_z, c]
            cores.append(push(here, here, sems, 6, i, to_core))
    for j in range(depth):
        from_z = (z - j + depth) % depth
        three[j].wait_recv()
        here = out.at[(3 - d) * depth + from_z, c]
        cores.append(push(here, here, sems, 7, j, to_core))
    for copy in cores:
        copy.wait_recv()
    for group in (along, one, two, three):
        for copy in group.values():
            copy.wait_send()
    for copy in cores:
        copy.wait_send()
    keep.wait()


def gather_kernel(depth, x_ref, down_ref, vdown_ref, out_ref, mats_ref, send, recv, wsend, wrecv, local):
    d, z, c, _, _ = place()
    greet(depth)
    spread_src = x_ref.at[c]
    own = [
        pltpu.make_async_copy(down_ref, mats_ref.at[0], local.at[1]),
        pltpu.make_async_copy(vdown_ref, mats_ref.at[1], local.at[2]),
    ]
    for copy in own:
        copy.start()
    other = [
        push(down_ref, mats_ref.at[2], (wsend, wrecv), 0, 0, (d, z, 1 - c)),
        push(vdown_ref, mats_ref.at[3], (wsend, wrecv), 0, 1, (d, z, 1 - c)),
    ]
    spread(depth, spread_src, out_ref, (send, recv), local.at[0])
    for copy in own + other:
        copy.wait()


def add_rows(rows, store, *terms):
    step = 16

    @pl.loop(0, rows // step)
    def _(i):
        at = pl.ds(pl.multiple_of(i * step, step), step)
        total = terms[0][at, :].astype(jnp.float32)
        for term in terms[1:]:
            total = total + term[at, :].astype(jnp.float32)
        store[at, :] = total.astype(store.dtype)


def reduce_kernel(
    depth, part_ref, out_ref, land_a, mine, send_b, land_b, send_c, land_c, own, total,
    rsend, rrecv, load, send, recv, local,
):
    d, z, c, first, second = place()
    rows = total.shape[0]
    order = list(range(1, depth)) + [0]
    loads = {}
    for k in order:
        zt = (z + k) % depth
        for slot, chip in ((1, second), (0, d)):
            loads[k, slot] = pltpu.make_async_copy(
                part_ref.at[chip * depth + zt], mine.at[k, slot], load.at[k, slot]
            )
            loads[k, slot].start()
    greet(depth)
    hop, turn, last = {}, {}, {}
    for k in order:
        zt = (z + k) % depth
        for slot, chip in ((1, 3 - d), (0, first)):
            hop[k, slot] = push(
                part_ref.at[chip * depth + zt], land_a.at[k, slot], (rsend, rrecv), slot, k, (first, z, c)
            )

    def finish(k):
        hop[k, 0].wait_recv()
        loads[k, 0].wait()
        turn[k].wait_recv()
        if k:
            add_rows(rows, send_c.at[k], mine.at[k, 0], land_a.at[k, 0], land_b.at[k])
            last[k] = push(
                send_c.at[k], land_c.at[k], (rsend, rrecv), 3, k, (d, (z + k) % depth, c)
            )
        else:
            add_rows(rows, own, mine.at[k, 0], land_a.at[k, 0], land_b.at[k])

    for i, k in enumerate(order):
        hop[k, 1].wait_recv()
        loads[k, 1].wait()
        add_rows(rows, send_b.at[k], mine.at[k, 1], land_a.at[k, 1])
        turn[k] = push(send_b.at[k], land_b.at[k], (rsend, rrecv), 2, k, (second, z, c))
        if i:
            finish(order[i - 1])
    finish(order[-1])
    for k in range(1, depth):
        last[k].wait_recv()
    add_rows(rows, total, own, *[land_c.at[k] for k in range(1, depth)])
    spread(depth, total, out_ref, (send, recv), local.at[0])
    for group in (hop, turn, last):
        for copy in group.values():
            copy.wait_send()


def gather_tokens(tokens, down_mat, vdown_mat):
    depth = lax.axis_size("expert")
    groups = lax.axis_size("dp") * depth
    count, width = tokens.shape
    half = count // 2
    dma = pltpu.SemaphoreType.DMA
    return pl.pallas_call(
        functools.partial(gather_kernel, depth),
        out_shape=(
            jax.ShapeDtypeStruct((groups, 2, half, width), jnp.bfloat16),
            jax.ShapeDtypeStruct((4,) + down_mat.shape, jnp.bfloat16),
        ),
        in_specs=[ANY, ANY, ANY],
        out_specs=(ANY, ANY),
        scratch_shapes=[dma((8, depth)), dma((8, depth)), dma((1, 2)), dma((1, 2)), dma((3,))],
        compiler_params=pltpu.CompilerParams(collective_id=0, has_side_effects=True),
    )(tokens.reshape(2, half, width), down_mat, vdown_mat)


def reduce_and_spread(part):
    depth = lax.axis_size("expert")
    groups, rows, width = part.shape
    dma = pltpu.SemaphoreType.DMA
    buf = lambda *lead: pltpu.VMEM(lead + (rows, width), jnp.bfloat16)
    return pl.pallas_call(
        functools.partial(reduce_kernel, depth),
        out_shape=jax.ShapeDtypeStruct((groups, 2, rows, width), jnp.bfloat16),
        in_specs=[ANY],
        out_specs=ANY,
        scratch_shapes=[
            buf(depth, 2), buf(depth, 2), buf(depth), buf(depth), buf(depth), buf(depth),
            pltpu.VMEM((rows, width), jnp.float32), buf(),
            dma((4, depth)), dma((4, depth)), dma((depth, 2)),
            dma((8, depth)), dma((8, depth)), dma((1,)),
        ],
        compiler_params=pltpu.CompilerParams(
            collective_id=1, has_side_effects=True, vmem_limit_bytes=48 * 1024 * 1024
        ),
    )(part)


def body(tokens, expert_ids, gates, token_weight, w_gate, w_up, w_down, v_gate, v_up, v_down):
    tok_count, width = tokens.shape
    picks = expert_ids.shape[1]
    groups = lax.axis_size("dp") * lax.axis_size("expert")
    half_tok = tok_count // 2
    core = lax.axis_index("tensor")
    me = lax.axis_index("dp") * lax.axis_size("expert") + lax.axis_index("expert")
    labels = jnp.arange(groups, dtype=jnp.int32)
    dense = jnp.sum(
        jnp.where(expert_ids[:, :, None] == labels, gates[:, :, None], 0.0), axis=1
    )
    table = jnp.concatenate([dense, token_weight[:, None]], axis=1)
    table = lax.all_gather(table, AXES, axis=0, tiled=True)
    gate_of = lax.dynamic_slice_in_dim(table, me, 1, 1)
    scale_of = gate_of * table[:, groups:]

    x_parts, mats = gather_tokens(tokens, w_down[0], v_down[0])
    x = x_parts.reshape(groups * tok_count, width)
    pre_gate = product(x, w_gate[0])
    pre_up = product(x, w_up[0])
    d_gate = product(x, v_gate[0])
    d_up = product(x, v_up[0])
    silu_g, slope_g = silu_parts(pre_gate)
    act_wide = silu_g * pre_up
    act = act_wide.astype(jnp.bfloat16)
    d_act = (slope_g * d_gate * pre_up + silu_g * d_up).astype(jnp.bfloat16)

    hidden = act.shape[1]
    both = jnp.concatenate([d_act, act], axis=1).reshape(groups, 2, half_tok, 2 * hidden)
    keep = lax.dynamic_index_in_dim(both, core, 1, keepdims=False)
    give = lax.dynamic_index_in_dim(both, 1 - core, 1, keepdims=False)
    got = lax.ppermute(give, "tensor", [(0, 1), (1, 0)])
    left = jnp.concatenate([keep, got], axis=2).reshape(groups * half_tok, 4 * hidden)
    gate_half = lax.dynamic_index_in_dim(
        gate_of.reshape(groups, 2, half_tok), core, 1, keepdims=False
    ).reshape(groups * half_tok, 1)
    part = (gate_half * product(left, mats.reshape(4 * hidden, width))).astype(jnp.bfloat16)

    dy_parts = reduce_and_spread(part.reshape(groups, half_tok, width))
    dy = dy_parts.reshape(groups * tok_count, width)
    tangent = lax.dynamic_slice(
        dy, (me * tok_count, core * (width // 2)), (tok_count, width // 2)
    )
    back = scale_of * lax.dot_general(
        dy, w_down[0], (((1,), (1,)), ((), ())), preferred_element_type=jnp.float32
    )
    grad_gate = (back * pre_up * slope_g).astype(jnp.bfloat16)
    grad_up = (back * silu_g).astype(jnp.bfloat16)
    act_scaled = (scale_of * act_wide).astype(jnp.bfloat16)
    factor = 1.0 / (tok_count * picks) ** 0.5
    return (
        (factor * contract_rows(x, grad_gate))[None],
        (factor * contract_rows(x, grad_up))[None],
        (factor * contract_rows(act_scaled, dy))[None],
        tangent,
    )


def solution(mesh):
    rows = P(AXES, None)
    wide = P(AXES, None, "tensor")
    tall = P(AXES, "tensor", None)
    in_specs = (rows, rows, rows, P(AXES), wide, wide, tall, wide, wide, tall)
    out_specs = (wide, wide, tall, P(AXES, "tensor"))
    return jax.shard_map(body, mesh=mesh, in_specs=in_specs, out_specs=out_specs, check_vma=False)
```

profile of v0, /device:TPU:27, one launch (start us, length us, event | category | flops | bytes accessed | tf_op | source)
XLA Modules:
  0.0 307.5 jit_solution(11043922241504141202)
XLA Ops:
  0.6 0.0 copy-start
  0.6 0.0 copy-start.8
  0.7 106.3 %shard_map.129 = (bf16[16,2,64,2048]{3,2,1,0:T(8,128)(2,1)}, bf16[4,384,2048]{2,1,0:T(8,128)(2,1)}) custom-call(bf16[2,64,2048]{2,1,0:T(8,128)(2,1)} %bitcast.53, bf16[384,2048]{1,0:T(8,128)(2,1)} %bitcast.51, bf16[384,2048]{1,0:T(8,128)(2,1)} %bitcast.50), custom_call_target="tpu_custom_call" | custom-call | tf_op jit(solution)/shard_map/pallas_call | solution.py:193
  107.0 0.0 copy-done.8
  107.0 0.0 copy-start.7
  107.0 0.0 copy-start.9
  107.0 6.8 %fusion.9 = f32[2048,384]{0,1:T(8,128)S(1)} fusion(bf16[2048,2048]{1,0:T(8,128)(2,1)} %bitcast.57, bf16[1,2048,384]{2,1,0:T(8,128)(2,1)S(1)} %copy-done.8), kind=kOutput, calls=%fused_computation.21 | convolution fusion | flops 3221225472 | bytes 13107200 | tf_op jit(solution)/shard_map/dot_general | solution.py:16
  113.8 0.0 copy-done.7
  113.8 0.0 copy-done.9
  113.8 0.0 copy-start.11
  113.9 5.3 %fusion.7 = f32[2048,384]{0,1:T(8,128)} fusion(bf16[2048,2048]{1,0:T(8,128)(2,1)S(1)} %bitcast.60, bf16[1,2048,384]{2,1,0:T(8,128)(2,1)S(1)} %copy-done.9), kind=kOutput, calls=%fused_computation.19 | convolution fusion | flops 3221225472 | bytes 13107200 | tf_op jit(solution)/shard_map/dot_general | solution.py:16
  119.2 0.0 copy-done
  119.2 0.0 copy-start.10
  119.2 9.1 %multiply_convert_fusion.7 = (bf16[2048,384]{0,1:T(8,128)(2,1)S(1)}, f32[2048,384]{0,1:T(8,128)}) fusion(f32[2048,384]{0,1:T(8,128)S(1)} %fusion.9, bf16[2048,2048]{1,0:T(8,128)(2,1)} %bitcast.58, bf16[1,2048,384]{2,1,0:T(8,128)(2,1)S(1)} %copy-done), kind=kOutput, calls=%fused_computation.26 | convolution fusion | flops 3225944064 | bytes 17825792 | tf_op jit(solution)/shard_map/dot_general | solution.py:16
  128.2 0.0 copy-done.11
  128.2 0.0 copy-done.10
  128.2 10.0 %add_convert_fusion = bf16[2048,384]{0,1:T(8,128)(2,1)S(1)} fusion(f32[2048,384]{0,1:T(8,128)} %get-tuple-element.13, f32[2048,384]{0,1:T(8,128)} %fusion.7, bf16[2048,2048]{1,0:T(8,128)(2,1)} %bitcast.59, bf16[1,2048,384]{2,1,0:T(8,128)(2,1)S(1)} %copy-done.10, f32[2048,384]{0,1:T(8,128)S(1)} %fusion.9), kind=kOutput, calls=%fused_computation.11 | convolution fusion | flops 3231449088 | bytes 20971520 | tf_op jit(solution)/shard_map/dot_general | solution.py:16
  138.2 0.4 pad_maximum_fusion
  138.7 2.8 copy.22
  141.5 0.0 copy-start.4
  141.5 2.1 constant_dynamic-slice_fusion
  143.6 1.0 collective-permute-start
  144.7 0.0 copy-done.4
  144.7 0.0 copy-done.5
  144.7 0.0 copy-done.6
  144.7 30.2 %all_gather.3 = f32[2048,17]{0,1:T(8,128)S(1)} all-gather(f32[128,17]{0,1:T(8,128)S(1)} %pad_maximum_fusion.1), channel_id=1, replica_groups=mesh['dp'=4,'expert'=4,'tensor'=2] {'dp','expert'}, dimensions={0}, use_global_device_ids=true | all-gather | bytes 147968 | tf_op jit(solution)/shard_map/all_gather | solution.py:240
  174.9 0.1 reshape.40
  175.0 0.1 mul.84
  175.1 0.0 collective-permute-done
  175.1 9.2 %multiply_convert_fusion = bf16[1024,2048]{1,0:T(8,128)(2,1)S(1)} fusion(bf16[1536,2048]{1,0:T(8,128)(2,1)} %bitcast.65, f32[1024]{0:T(1024)S(1)} %mul.84, bf16[1024,768]{1,0:T(8,128)(2,1)} %bitcast.13, bf16[1024,768]{1,0:T(8,128)(2,1)S(1)} %bitcast.52), kind=kOutput, calls=%fused_computation | convolution fusion | flops 6452936704 | bytes 13635584 | tf_op jit(solution)/shard_map/dot_general | solution.py:16
  184.3 0.0 copy-start.3
  184.4 95.9 %shard_map.130 = bf16[16,2,64,2048]{3,2,1,0:T(8,128)(2,1)} custom-call(bf16[16,64,2048]{2,1,0:T(8,128)(2,1)S(1)} %bitcast.45), custom_call_target="tpu_custom_call" | custom-call | tf_op jit(solution)/shard_map/pallas_call | solution.py:211
  280.3 0.0 copy-done.3
  280.3 0.0 copy-start.2
  280.3 0.0 copy-start.12
  280.3 0.0 copy-start.13
  280.3 0.0 slice-start
  280.3 6.7 %convolution_multiply_fusion = f32[2048,384]{0,1:T(8,128)S(1)} fusion(bf16[2048,2048]{1,0:T(8,128)(2,1)} %bitcast.47, f32[2048]{0:T(1024)S(1)} %bitcast.54, bf16[1,384,2048]{2,1,0:T(8,128)(2,1)S(1)} %copy-done.3), kind=kOutput, calls=%fused_computation.15 | convolution fusion | flops 3222011904 | bytes 13115392 | tf_op jit(solution)/shard_map/dot_general | solution.py:271
  287.0 0.0 copy-done.2
  287.0 0.0 copy-done.12
  287.0 0.9 copy-done.13
  287.9 5.4 %multiply_bitcast_fusion = f32[1,384,2048]{2,1,0:T(8,128)} fusion(bf16[2048,2048]{1,0:T(8,128)(2,1)S(1)} %bitcast.48, f32[2048]{0:T(1024)S(1)} %bitcast.55, f32[2048,384]{0,1:T(8,128)S(1)} %copy-done.13, f32[2048,384]{0,1:T(8,128)S(1)} %copy-done.12), kind=kOutput, calls=%fused_computation.5 | convolution fusion | flops 3227516928 | bytes 17833984 | tf_op jit(solution)/shard_map/dot_general | solution.py:20
  293.3 0.0 slice-done
  293.3 0.0 slice-done.1
  293.3 6.7 %multiply_bitcast_fusion.2 = f32[1,2048,384]{2,1,0:T(8,128)} fusion(bf16[2048,2048]{1,0:T(8,128)(2,1)S(1)} %bitcast.63, f32[2048,384]{0,1:T(8,128)S(1)} %convolution_multiply_fusion, f32[2048,384]{0,1:T(8,128)S(1)} %copy-done.13, f32[2048,384]{0,1:T(8,128)S(1)} %copy-done.12), kind=kOutput, calls=%fused_computation.9 | convolution fusion | flops 3229876224 | bytes 20971520 | tf_op jit(solution)/shard_map/dot_general | solution.py:20
  300.0 6.7 %multiply_bitcast_fusion.1 = f32[1,2048,384]{2,1,0:T(8,128)} fusion(bf16[2048,2048]{1,0:T(8,128)(2,1)S(1)} %bitcast.64, f32[2048,384]{0,1:T(8,128)S(1)} %convolution_multiply_fusion, f32[2048,384]{0,1:T(8,128)S(1)} %copy-done.12), kind=kOutput, calls=%fused_computation.7 | convolution fusion | flops 3226730496 | bytes 17825792 | tf_op jit(solution)/shard_map/dot_general | solution.py:20
  306.8 0.7 dynamic_slice.21
  307.5 0.0 copy-done.1
  (9 shorter events, 0.1 us)
Async XLA Ops:
  0.6 118.5 %copy-start = (bf16[1,2048,384]{2,1,0:T(8,128)(2,1)S(1)}, bf16[1,2048,384]{2,1,0:T(8,128)(2,1)}, u32[]{:S(2)}) copy-start(bf16[1,2048,384]{2,1,0:T(8,128)(2,1)} %param.15) | copy-start | bytes 4718596
  0.6 106.3 %copy-start.8 = (bf16[1,2048,384]{2,1,0:T(8,128)(2,1)S(1)}, bf16[1,2048,384]{2,1,0:T(8,128)(2,1)}, u32[]{:S(2)}) copy-start(bf16[1,2048,384]{2,1,0:T(8,128)(2,1)} %param.14) | copy-start | bytes 4718596
  107.0 6.9 %copy-start.7 = (bf16[16,2,64,2048]{3,2,1,0:T(8,128)(2,1)S(1)}, bf16[16,2,64,2048]{3,2,1,0:T(8,128)(2,1)}, u32[]{:S(2)}) copy-start(bf16[16,2,64,2048]{3,2,1,0:T(8,128)(2,1)} %get-tuple-element.6) | copy-start | bytes 25165828
  107.0 6.9 %copy-start.9 = (bf16[1,2048,384]{2,1,0:T(8,128)(2,1)S(1)}, bf16[1,2048,384]{2,1,0:T(8,128)(2,1)}, u32[]{:S(2)}) copy-start(bf16[1,2048,384]{2,1,0:T(8,128)(2,1)} %param.17) | copy-start | bytes 4718596
  113.8 14.4 %copy-start.11 = (f32[2048,384]{0,1:T(8,128)}, f32[2048,384]{0,1:T(8,128)S(1)}, u32[]{:S(2)}) copy-start(f32[2048,384]{0,1:T(8,128)S(1)} %fusion.9) | copy-start | bytes 9437188
  119.2 9.1 %copy-start.10 = (bf16[1,2048,384]{2,1,0:T(8,128)(2,1)S(1)}, bf16[1,2048,384]{2,1,0:T(8,128)(2,1)}, u32[]{:S(2)}) copy-start(bf16[1,2048,384]{2,1,0:T(8,128)(2,1)} %param.18) | copy-start | bytes 4718596
  141.5 3.2 %copy-start.4 = (f32[128,8]{0,1:T(8,128)S(1)}, f32[128,8]{0,1:T(8,128)}, u32[]{:S(2)}) copy-start(f32[128,8]{0,1:T(8,128)} %param.12) | copy-start | bytes 12292
  141.5 3.2 %copy-start.5 = (s32[128,8]{0,1:T(8,128)S(1)}, s32[128,8]{0,1:T(8,128)}, u32[]{:S(2)}) copy-start(s32[128,8]{0,1:T(8,128)} %param.11) | copy-start | bytes 12292
  141.5 3.2 %copy-start.6 = (f32[128]{0:T(128)S(1)}, f32[128]{0:T(128)}, u32[]{:S(2)}) copy-start(f32[128]{0:T(128)} %param.13) | copy-start | bytes 1540
  143.6 31.5 %collective-permute-start = (bf16[16,64,768]{2,1,0:T(8,128)(2,1)S(1)}, bf16[16,64,768]{2,1,0:T(8,128)(2,1)}, u32[]{:S(2)}, u32[]{:S(2)}) collective-permute-start(bf16[16,64,768]{2,1,0:T(8,128)(2,1)S(1)} %get-tuple-element.9), channel_id=1, source_target_pairs={{0,1},{1,0},{2,3},{3,2},{4,5},{5,4},{6,7},{7,6},{8,9},{9,8},{10,11... | collective-permute-start | bytes 4718600 | tf_op jit(solution)/shard_map/ppermute | solution.py:259
  184.3 95.9 %copy-start.3 = (bf16[1,384,2048]{2,1,0:T(8,128)(2,1)S(1)}, bf16[1,384,2048]{2,1,0:T(8,128)(2,1)}, u32[]{:S(2)}) copy-start(bf16[1,384,2048]{2,1,0:T(8,128)(2,1)} %param.16) | copy-start | bytes 4718596
  280.3 6.7 %copy-start.2 = (bf16[16,2,64,2048]{3,2,1,0:T(8,128)(2,1)S(1)}, bf16[16,2,64,2048]{3,2,1,0:T(8,128)(2,1)}, u32[]{:S(2)}) copy-start(bf16[16,2,64,2048]{3,2,1,0:T(8,128)(2,1)} %shard_map.130) | copy-start | bytes 25165828
  280.3 6.7 %copy-start.12 = (f32[2048,384]{0,1:T(8,128)S(1)}, f32[2048,384]{0,1:T(8,128)}, u32[]{:S(2)}) copy-start(f32[2048,384]{0,1:T(8,128)} %copy-done.11) | copy-start | bytes 9437188
  280.3 7.6 %copy-start.13 = (f32[2048,384]{0,1:T(8,128)S(1)}, f32[2048,384]{0,1:T(8,128)}, u32[]{:S(2)}) copy-start(f32[2048,384]{0,1:T(8,128)} %get-tuple-element.13) | copy-start | bytes 9437188
  280.3 13.0 %slice-start = ((s8[8388608]{0:T(1024)(128)(4,1)}), s8[4194304]{0:T(1024)(128)(4,1)S(1)}, s32[]{:S(2)}) async-start(s8[8388608]{0:T(1024)(128)(4,1)} %bitcast.61), calls=%async_computation | async-start | bytes 8388608
  287.9 5.4 %slice-start.1 = ((s8[8388608]{0:T(1024)(128)(4,1)}), s8[4194304]{0:T(1024)(128)(4,1)S(1)}, s32[]{:S(2)}) async-start(s8[8388608]{0:T(1024)(128)(4,1)} %bitcast.61), calls=%async_computation.1 | async-start | bytes 8388608
  300.0 7.4 %copy-start.1 = (bf16[1,2048,384]{2,1,0:T(8,128)(2,1)S(1)}, bf16[1,2048,384]{2,1,0:T(8,128)(2,1)}, u32[]{:S(2)}) copy-start(bf16[1,2048,384]{2,1,0:T(8,128)(2,1)} %param.15) | copy-start | bytes 4718596
where the time goes:
time: 310 us; the launch traced here: 307 us
  Pallas kernels  202 us (65%)
  matrix products  65.9 us (21%)
  blocking collectives  30.2 us (10%)
  local copies, waits for them, and re-layouts  6.82 us (2%)
    pallas_call x1, Pallas kernels, gather_tokens(): pl.pallas_call(functools.partial(gather_kernel, depth), out_shape=(jax.Sh...  106 us
    pallas_call x1, Pallas kernels, reduce_and_spread(): pl.pallas_call(functools.partial(reduce_kernel, depth), out_shape=jax.Sha...  95.9 us
    dot_general x5, matrix products, product(): return jnp.dot(left, right, preferred_element_type=jnp.float32)  40.4 us
    all_gather x1, blocking collectives, body(): table = lax.all_gather(table, AXES, axis=0, tiled=True)  30.2 us
    dot_general x3, matrix products, contract_rows(): lax.dot_general(left, right, (((0,), (0,)), ((), ())), preferred_element_...  18.8 us
    dot_general x1, matrix products, body(): lax.dot_general(dy, w_down[0], (((1,), (1,)), ((), ())), preferred_elemen...  6.65 us
  transfers between devices with their start and end apart: 1, of which 0 were waited for; matrix products, arithmetic and copies ran while one was open for 0% of the time, Pallas kernels for 0%

commit v1 on v0

--- a/solution.py
+++ b/solution.py
@@ -56,21 +56,36 @@
     return copy
 
 
-def spread(depth, src, out, sems, local_sem):
+def spread(depth, src, out, sems, local_sem, small=None):
     d, z, c, first, second = place()
     to_first, to_second, to_core = (first, z, c), (second, z, c), (d, z, 1 - c)
     sent, along, one, two, three, cores = [], {}, {}, {}, {}, []
     spot = out.at[d * depth + z, c]
     keep = pltpu.make_async_copy(src, spot, local_sem)
     keep.start()
+    extra, flat = {}, None
+    if small is not None:
+        flat, all_flat = small
+        flat_spot = all_flat.at[d * depth + z]
+        flat_keep = pltpu.make_async_copy(flat, flat_spot, local_sem)
     for k in range(1, depth):
-        along[k] = push(src, spot, sems, 0, k, (d, (z + k) % depth, c))
+        to_z = (d, (z + k) % depth, c)
+        if flat is not None:
+            extra[0, k] = push(flat, flat_spot, sems, 8, k, to_z)
+        along[k] = push(src, spot, sems, 0, k, to_z)
     for j in range(depth + 1):
         if j < depth:
             from_z = (z - j + depth) % depth
             here = out.at[d * depth + from_z, c]
             if j:
                 along[j].wait_recv()
+            if flat is not None:
+                if j:
+                    extra[0, j].wait_recv()
+                flat_here = all_flat.at[d * depth + from_z]
+                flat_body = flat_here if j else flat
+                extra[1, j] = push(flat_body, flat_here, sems, 9, j, to_first)
+                extra[2, j] = push(flat_body, flat_here, sems, 10, j, to_second)
             body = here if j else src
             one[j] = push(body, here, sems, 1, j, to_first)
             two[j] = push(body, here, sems, 2, j, to_second)
@@ -81,6 +96,10 @@
             one[i].wait_recv()
             here = out.at[first * depth + from_z, c]
             three[i] = push(here, here, sems, 3, i, to_second)
+            if flat is not None:
+                extra[1, i].wait_recv()
+                flat_here = all_flat.at[first * depth + from_z]
+                extra[3, i] = push(flat_here, flat_here, sems, 11, i, to_second)
             cores.append(push(here, here, sems, 5, i, to_core))
             two[i].wait_recv()
             here = out.at[second * depth + from_z, c]
@@ -98,25 +117,19 @@
     for copy in cores:
         copy.wait_send()
     keep.wait()
-
-
-def gather_kernel(depth, x_ref, down_ref, vdown_ref, out_ref, mats_ref, send, recv, wsend, wrecv, local):
-    d, z, c, _, _ = place()
+    if flat is not None:
+        flat_keep.start()
+        for (row, _), copy in extra.items():
+            if row >= 2:
+                copy.wait_recv()
+            copy.wait_send()
+        flat_keep.wait()
+
+
+def gather_kernel(depth, x_ref, table_ref, out_ref, tables_ref, send, recv, local):
     greet(depth)
-    spread_src = x_ref.at[c]
-    own = [
-        pltpu.make_async_copy(down_ref, mats_ref.at[0], local.at[1]),
-        pltpu.make_async_copy(vdown_ref, mats_ref.at[1], local.at[2]),
-    ]
-    for copy in own:
-        copy.start()
-    other = [
-        push(down_ref, mats_ref.at[2], (wsend, wrecv), 0, 0, (d, z, 1 - c)),
-        push(vdown_ref, mats_ref.at[3], (wsend, wrecv), 0, 1, (d, z, 1 - c)),
-    ]
-    spread(depth, spread_src, out_ref, (send, recv), local.at[0])
-    for copy in own + other:
-        copy.wait()
+    c = lax.axis_index("tensor")
+    spread(depth, x_ref.at[c], out_ref, (send, recv), local.at[0], (table_ref, tables_ref))
 
 
 def add_rows(rows, store, *terms):
@@ -184,7 +197,7 @@
             copy.wait_send()
 
 
-def gather_tokens(tokens, down_mat, vdown_mat):
+def gather_tokens(tokens, table):
     depth = lax.axis_size("expert")
     groups = lax.axis_size("dp") * depth
     count, width = tokens.shape
@@ -194,18 +207,21 @@
         functools.partial(gather_kernel, depth),
         out_shape=(
             jax.ShapeDtypeStruct((groups, 2, half, width), jnp.bfloat16),
-            jax.ShapeDtypeStruct((4,) + down_mat.shape, jnp.bfloat16),
+            jax.ShapeDtypeStruct((groups,) + table.shape, jnp.float32),
         ),
-        in_specs=[ANY, ANY, ANY],
+        in_specs=[ANY, ANY],
         out_specs=(ANY, ANY),
-        scratch_shapes=[dma((8, depth)), dma((8, depth)), dma((1, 2)), dma((1, 2)), dma((3,))],
-        compiler_params=pltpu.CompilerParams(collective_id=0, has_side_effects=True),
-    )(tokens.reshape(2, half, width), down_mat, vdown_mat)
+        scratch_shapes=[dma((12, depth)), dma((12, depth)), dma((1,))],
+        compiler_params=pltpu.CompilerParams(
+            collective_id=0, has_side_effects=True, vmem_limit_bytes=2 * 1024 * 1024
+        ),
+    )(tokens.reshape(2, half, width), table)
 
 
 def reduce_and_spread(part):
     depth = lax.axis_size("expert")
     groups, rows, width = part.shape
+    room = (8 * depth + 3) * rows * width * 2 + 4 * 1024 * 1024
     dma = pltpu.SemaphoreType.DMA
     buf = lambda *lead: pltpu.VMEM(lead + (rows, width), jnp.bfloat16)
     return pl.pallas_call(
@@ -220,7 +236,7 @@
             dma((8, depth)), dma((8, depth)), dma((1,)),
         ],
         compiler_params=pltpu.CompilerParams(
-            collective_id=1, has_side_effects=True, vmem_limit_bytes=48 * 1024 * 1024
+            collective_id=1, has_side_effects=True, vmem_limit_bytes=room
         ),
     )(part)
 
@@ -236,12 +252,20 @@
     dense = jnp.sum(
         jnp.where(expert_ids[:, :, None] == labels, gates[:, :, None], 0.0), axis=1
     )
-    table = jnp.concatenate([dense, token_weight[:, None]], axis=1)
-    table = lax.all_gather(table, AXES, axis=0, tiled=True)
-    gate_of = lax.dynamic_slice_in_dim(table, me, 1, 1)
-    scale_of = gate_of * table[:, groups:]
-
-    x_parts, mats = gather_tokens(tokens, w_down[0], v_down[0])
+    pad = -(groups + 1) % 8
+    table = jnp.concatenate(
+        [dense.T, token_weight[None], jnp.zeros((pad, tok_count), jnp.float32)], axis=0
+    )
+    x_parts, tables = gather_tokens(tokens, table)
+    gate_of = lax.dynamic_index_in_dim(tables, me, 1, keepdims=False).reshape(-1, 1)
+    scale_of = gate_of * tables[:, groups].reshape(-1, 1)
+    down_mat, vdown_mat = w_down[0], v_down[0]
+    x_parts, down_send, vdown_send = lax.optimization_barrier((x_parts, down_mat, vdown_mat))
+    swap = [(0, 1), (1, 0)]
+    down_other = lax.ppermute(down_send, "tensor", swap)
+    vdown_other = lax.ppermute(vdown_send, "tensor", swap)
+    mats = jnp.concatenate([down_mat, vdown_mat, down_other, vdown_other], axis=0)
+
     x = x_parts.reshape(groups * tok_count, width)
     pre_gate = product(x, w_gate[0])
     pre_up = product(x, w_up[0])
@@ -256,12 +280,12 @@
     both = jnp.concatenate([d_act, act], axis=1).reshape(groups, 2, half_tok, 2 * hidden)
     keep = lax.dynamic_index_in_dim(both, core, 1, keepdims=False)
     give = lax.dynamic_index_in_dim(both, 1 - core, 1, keepdims=False)
-    got = lax.ppermute(give, "tensor", [(0, 1), (1, 0)])
+    got = lax.ppermute(give, "tensor", swap)
     left = jnp.concatenate([keep, got], axis=2).reshape(groups * half_tok, 4 * hidden)
     gate_half = lax.dynamic_index_in_dim(
         gate_of.reshape(groups, 2, half_tok), core, 1, keepdims=False
     ).reshape(groups * half_tok, 1)
-    part = (gate_half * product(left, mats.reshape(4 * hidden, width))).astype(jnp.bfloat16)
+    part = (gate_half * product(left, mats)).astype(jnp.bfloat16)
 
     dy_parts = reduce_and_spread(part.reshape(groups, half_tok, width))
     dy = dy_parts.reshape(groups * tok_count, width)

time: 310 us -> 219 us (0.71)
  Pallas kernels: 202 us -> 141 us
  blocking collectives: 30.2 us -> 0 us
  matrix products: 65.9 us -> 57.6 us
  local copies, waits for them, and re-layouts: 6.82 us -> 12.2 us
  waiting for transfers between devices: 0.01 us -> 3.25 us
  other arithmetic: 0.49 us -> 3.6 us
    pallas_call x1, Pallas kernels: 106 us -> 51.3 us  [gather_tokens(): pl.pallas_call(functools.partial(gather_kernel, depth), out_shape=(jax.Sh...]
    all_gather x1 -> x0, blocking collectives: 30.2 us -> none  [body(): table = lax.all_gather(table, AXES, axis=0, tiled=True)]
    pallas_call x1, Pallas kernels: 95.9 us -> 89.7 us  [reduce_and_spread(): pl.pallas_call(functools.partial(reduce_kernel, depth), out_shape=jax.Sha...]
    dot_general x5, matrix products: 40.4 us -> 35.1 us  [product(): return jnp.dot(left, right, preferred_element_type=jnp.float32)]
    unnamed x32 -> x24, local copies, waits for them, and re-layouts: 1 us -> 4.31 us
    ppermute x1 -> x3, waiting for transfers between devices: 0.01 us -> 3.25 us  [the longest x1 3.24 us: body(): got = lax.ppermute(give, 'tensor', swap)]
    dot_general x1, matrix products: 6.65 us -> 3.47 us  [body(): lax.dot_general(dy, w_down[0], (((1,), (1,)), ((), ())), preferred_elemen...]
  transfers between devices with their start and end apart: 1 -> 3, of which waited for: 0 -> 1; matrix products, arithmetic and copies ran while one was open for 0% -> 16% of each run, Pallas kernels for 0% -> 0%
where the time goes in v1:
time: 219 us
  Pallas kernels  141 us (64%)
  matrix products  57.6 us (26%)
  local copies, waits for them, and re-layouts  12.2 us (6%)
  other arithmetic  3.6 us (2%)
  waiting for transfers between devices  3.25 us (1%)
    pallas_call x1, Pallas kernels, reduce_and_spread(): pl.pallas_call(functools.partial(reduce_kernel, depth), out_shape=jax.Sha...  89.7 us
    pallas_call x1, Pallas kernels, gather_tokens(): pl.pallas_call(functools.partial(gather_kernel, depth), out_shape=(jax.Sh...  51.3 us
    dot_general x5, matrix products, product(): return jnp.dot(left, right, preferred_element_type=jnp.float32)  35.1 us
    dot_general x3, matrix products, contract_rows(): lax.dot_general(left, right, (((0,), (0,)), ((), ())), preferred_element_...  19 us
    concatenate x1, local copies, waits for them, and re-layouts, body(): jnp.concatenate([d_act, act], axis=1)  4.72 us
  transfers between devices with their start and end apart: 3, of which 1 were waited for; matrix products, arithmetic and copies ran while one was open for 16% of the time, Pallas kernels for 0%

profile of v1, /device:TPU:27, one launch (start us, length us, event | category | flops | bytes accessed | tf_op | source)
XLA Modules:
  0.0 219.0 jit_solution(14660745560215101274)
XLA Ops:
  0.6 0.0 copy-start
  0.7 0.1 pad.10.clone
  0.7 0.8 select_reduce_fusion
  1.6 0.7 maximum_maximum_fusion.table_ref
  2.3 1.0 copy-done.2
  3.3 51.3 %shard_map.129 = (bf16[16,2,64,2048]{3,2,1,0:T(8,128)(2,1)S(1)}, f32[16,24,128]{2,1,0:T(8,128)S(1)}) custom-call(bf16[2,64,2048]{2,1,0:T(8,128)(2,1)S(1)} %bitcast.48, f32[24,128]{1,0:T(8,128)S(1)} %maximum_maximum_fusion.table_ref), custom_call_target="tpu_custom_call" | custom-call | tf_op jit(solution)/shard_map/pallas_call | solution.py:206
  54.7 0.0 copy-start.3
  54.7 3.2 %copy-done.3 = bf16[16,2,64,2048]{3,2,1,0:T(8,128)(2,1)} copy-done((bf16[16,2,64,2048]{3,2,1,0:T(8,128)(2,1)}, bf16[16,2,64,2048]{3,2,1,0:T(8,128)(2,1)S(1)}, u32[]{:S(2)}) %copy-start.3) | copy-done | bytes 8388632
  57.9 0.1 collective-permute-start.1
  57.9 0.4 collective-permute-start.2
  58.4 0.0 copy-start.4
  58.4 0.0 copy-start.5
  58.4 6.7 %fusion.19 = f32[2048,384]{0,1:T(8,128)S(1)} fusion(bf16[2048,2048]{1,0:T(8,128)(2,1)} %bitcast.49, bf16[1,2048,384]{2,1,0:T(8,128)(2,1)} %param.14), kind=kOutput, calls=%fused_computation.29 | convolution fusion | flops 3221225472 | bytes 13107200 | tf_op jit(solution)/shard_map/dot_general | solution.py:16
  65.1 0.0 copy-done.4
  65.1 0.0 copy-done.5
  65.1 0.0 copy-start.7
  65.1 5.2 %fusion.17 = f32[2048,384]{0,1:T(8,128)} fusion(bf16[2048,2048]{1,0:T(8,128)(2,1)S(1)} %bitcast.50, bf16[1,2048,384]{2,1,0:T(8,128)(2,1)S(1)} %copy-done.5), kind=kOutput, calls=%fused_computation.27 | convolution fusion | flops 3221225472 | bytes 13107200 | tf_op jit(solution)/shard_map/dot_general | solution.py:16
  70.3 0.0 copy-done.7
  70.3 0.0 copy-done
  70.3 5.7 %multiply_convert_fusion.7 = (bf16[2048,384]{0,1:T(8,128)(2,1)S(1)}, f32[2048,384]{0,1:T(8,128)}) fusion(f32[2048,384]{0,1:T(8,128)S(1)} %fusion.19, bf16[2048,2048]{1,0:T(8,128)(2,1)S(1)} %bitcast.51, bf16[1,2048,384]{2,1,0:T(8,128)(2,1)S(1)} %copy-done), kind=kOutput, calls=%fused_computation.34 | convolution fusion | flops 3225944064 | bytes 17825792 | tf_op jit(solution)/shard_map/dot_general | solution.py:16
  76.0 8.3 %add_convert_fusion = bf16[2048,384]{0,1:T(8,128)(2,1)S(1)} fusion(f32[2048,384]{0,1:T(8,128)} %get-tuple-element.19, f32[2048,384]{0,1:T(8,128)} %fusion.17, bf16[2048,2048]{1,0:T(8,128)(2,1)S(1)} %bitcast.52, bf16[1,2048,384]{2,1,0:T(8,128)(2,1)} %param.18, f32[2048,384]{0,1:T(8,128)} %copy-done.7), kind=kOutput, calls=%fused_computation.19 | convolution fusion | flops 3231449088 | bytes 20971520 | tf_op jit(solution)/shard_map/dot_general | solution.py:16
  84.3 2.0 pad_maximum_fusion
  86.3 4.7 %copy.21 = bf16[2048,768]{1,0:T(8,128)(2,1)} copy(bf16[2048,768]{0,1:T(8,128)(2,1)} %pad_maximum_fusion) | data formatting | bytes 6291456 | tf_op jit(solution)/shard_map/concatenate | solution.py:280
  91.0 2.2 constant_dynamic-slice_fusion
  93.2 0.1 collective-permute-start
  93.4 0.1 reshape_reshape.3
  93.5 0.1 mul.90
  93.5 0.0 collective-permute-done.1
  93.5 0.0 collective-permute-done.2
  93.5 3.2 %collective-permute-done = bf16[16,64,768]{2,1,0:T(8,128)(2,1)} collective-permute-done((bf16[16,64,768]{2,1,0:T(8,128)(2,1)S(1)}, bf16[16,64,768]{2,1,0:T(8,128)(2,1)}, u32[]{:S(2)}, u32[]{:S(2)}) %collective-permute-start) | collective-permute-done | bytes 1572896 | tf_op jit(solution)/shard_map/ppermute | solution.py:283
  96.8 9.3 %multiply_convert_fusion = bf16[1024,2048]{1,0:T(8,128)(2,1)S(1)} fusion(f32[1024]{0:T(1024)S(1)} %mul.90, bf16[384,2048]{1,0:T(8,128)(2,1)} %collective-permute-done.2, bf16[384,2048]{1,0:T(8,128)(2,1)} %collective-permute-done.1, bf16[384,2048]{1,0:T(8,128)(2,1)} %bitcast.64, bf16[384,2048]{1,0:T(8,128)(2,1)} %bitcast.66, bf16[1024,768]{1,0:T(8,128)(2,1)} %bitcast.14, ...), kind=kOutput, calls=%fused_computation | convolution fusion | flops 6478102528 | bytes 13635584 | tf_op jit(solution)/shard_map/dot_general | solution.py:16
  106.0 0.0 copy-start.6
  106.1 89.7 %shard_map.130 = bf16[16,2,64,2048]{3,2,1,0:T(8,128)(2,1)S(1)} custom-call(bf16[16,64,2048]{2,1,0:T(8,128)(2,1)S(1)} %bitcast.47), custom_call_target="tpu_custom_call" | custom-call | tf_op jit(solution)/shard_map/pallas_call | solution.py:227
  195.8 0.0 copy-done.6
  195.8 0.0 copy-start.8
  195.8 0.0 copy-start.9
  195.8 0.0 slice-start
  195.8 3.5 %convolution_multiply_fusion = f32[2048,384]{0,1:T(8,128)S(1)} fusion(bf16[2048,2048]{1,0:T(8,128)(2,1)S(1)} %bitcast.44, f32[2048]{0:T(1024)S(1)} %bitcast.60, bf16[1,384,2048]{2,1,0:T(8,128)(2,1)S(1)} %copy-done.6), kind=kOutput, calls=%fused_computation.23 | convolution fusion | flops 3222011904 | bytes 13115392 | tf_op jit(solution)/shard_map/dot_general | solution.py:295
  199.3 0.0 copy-done.8
  199.3 0.0 copy-done.9
  199.3 0.0 slice-start.1
  199.3 5.3 %multiply_bitcast_fusion = f32[1,384,2048]{2,1,0:T(8,128)} fusion(bf16[2048,2048]{1,0:T(8,128)(2,1)S(1)} %bitcast.45, f32[2048]{0:T(1024)S(1)} %bitcast.61, f32[2048,384]{0,1:T(8,128)S(1)} %copy-done.9, f32[2048,384]{0,1:T(8,128)S(1)} %copy-done.8), kind=kOutput, calls=%fused_computation.13 | convolution fusion | flops 3227516928 | bytes 17833984 | tf_op jit(solution)/shard_map/dot_general | solution.py:20
  204.6 0.0 slice-done
  204.6 0.0 slice-done.1
  204.6 6.7 %multiply_bitcast_fusion.2 = f32[1,2048,384]{2,1,0:T(8,128)} fusion(bf16[2048,2048]{1,0:T(8,128)(2,1)S(1)} %bitcast.55, f32[2048,384]{0,1:T(8,128)S(1)} %convolution_multiply_fusion, f32[2048,384]{0,1:T(8,128)S(1)} %copy-done.9, f32[2048,384]{0,1:T(8,128)S(1)} %copy-done.8), kind=kOutput, calls=%fused_computation.17 | convolution fusion | flops 3229876224 | bytes 20971520 | tf_op jit(solution)/shard_map/dot_general | solution.py:20
  211.4 6.9 %multiply_bitcast_fusion.1 = f32[1,2048,384]{2,1,0:T(8,128)} fusion(bf16[2048,2048]{1,0:T(8,128)(2,1)S(1)} %bitcast.56, f32[2048,384]{0,1:T(8,128)S(1)} %convolution_multiply_fusion, f32[2048,384]{0,1:T(8,128)S(1)} %copy-done.8), kind=kOutput, calls=%fused_computation.15 | convolution fusion | flops 3226730496 | bytes 17825792 | tf_op jit(solution)/shard_map/dot_general | solution.py:20
  218.3 0.7 dynamic_slice.22
  219.0 0.0 copy-done.1
  (6 shorter events, 0.1 us)
Async XLA Ops:
  0.6 69.7 %copy-start = (bf16[1,2048,384]{2,1,0:T(8,128)(2,1)S(1)}, bf16[1,2048,384]{2,1,0:T(8,128)(2,1)}, u32[]{:S(2)}) copy-start(bf16[1,2048,384]{2,1,0:T(8,128)(2,1)} %param.15) | copy-start | bytes 4718596
  2.3 1.0 copy-start.2
  54.7 3.2 %copy-start.3 = (bf16[16,2,64,2048]{3,2,1,0:T(8,128)(2,1)}, bf16[16,2,64,2048]{3,2,1,0:T(8,128)(2,1)S(1)}, u32[]{:S(2)}) copy-start(bf16[16,2,64,2048]{3,2,1,0:T(8,128)(2,1)S(1)} %get-tuple-element.10) | copy-start | bytes 25165828
  57.9 35.7 %collective-permute-start.1 = (bf16[384,2048]{1,0:T(8,128)(2,1)}, bf16[384,2048]{1,0:T(8,128)(2,1)}, u32[]{:S(2)}, u32[]{:S(2)}) collective-permute-start(bf16[384,2048]{1,0:T(8,128)(2,1)} %bitcast.65), channel_id=1, source_target_pairs={{0,1},{1,0},{2,3},{3,2},{4,5},{5,4},{6,7},{7,6},{8,9},{9,8},{10,11... | collective-permute-start | bytes 4718600 | tf_op jit(solution)/shard_map/ppermute | solution.py:265
  57.9 35.6 %collective-permute-start.2 = (bf16[384,2048]{1,0:T(8,128)(2,1)}, bf16[384,2048]{1,0:T(8,128)(2,1)}, u32[]{:S(2)}, u32[]{:S(2)}) collective-permute-start(bf16[384,2048]{1,0:T(8,128)(2,1)} %bitcast.63), channel_id=1, source_target_pairs={{0,1},{1,0},{2,3},{3,2},{4,5},{5,4},{6,7},{7,6},{8,9},{9,8},{10,11... | collective-permute-start | bytes 4718600 | tf_op jit(solution)/shard_map/ppermute | solution.py:266
  58.4 6.7 %copy-start.4 = (bf16[16,2,64,2048]{3,2,1,0:T(8,128)(2,1)S(1)}, bf16[16,2,64,2048]{3,2,1,0:T(8,128)(2,1)}, u32[]{:S(2)}) copy-start(bf16[16,2,64,2048]{3,2,1,0:T(8,128)(2,1)} %copy-done.3) | copy-start | bytes 25165828
  58.4 6.7 %copy-start.5 = (bf16[1,2048,384]{2,1,0:T(8,128)(2,1)S(1)}, bf16[1,2048,384]{2,1,0:T(8,128)(2,1)}, u32[]{:S(2)}) copy-start(bf16[1,2048,384]{2,1,0:T(8,128)(2,1)} %param.17) | copy-start | bytes 4718596
  65.1 5.2 %copy-start.7 = (f32[2048,384]{0,1:T(8,128)}, f32[2048,384]{0,1:T(8,128)S(1)}, u32[]{:S(2)}) copy-start(f32[2048,384]{0,1:T(8,128)S(1)} %fusion.19) | copy-start | bytes 9437188
  93.2 3.6 %collective-permute-start = (bf16[16,64,768]{2,1,0:T(8,128)(2,1)S(1)}, bf16[16,64,768]{2,1,0:T(8,128)(2,1)}, u32[]{:S(2)}, u32[]{:S(2)}) collective-permute-start(bf16[16,64,768]{2,1,0:T(8,128)(2,1)S(1)} %get-tuple-element.15), channel_id=1, source_target_pairs={{0,1},{1,0},{2,3},{3,2},{4,5},{5,4},{6,7},{7,6},{8,9},{9,8},{10,11... | collective-permute-start | bytes 4718600 | tf_op jit(solution)/shard_map/ppermute | solution.py:283
  106.0 89.7 %copy-start.6 = (bf16[1,384,2048]{2,1,0:T(8,128)(2,1)S(1)}, bf16[1,384,2048]{2,1,0:T(8,128)(2,1)}, u32[]{:S(2)}) copy-start(bf16[1,384,2048]{2,1,0:T(8,128)(2,1)} %param.16) | copy-start | bytes 4718596
  195.8 3.5 %copy-start.8 = (f32[2048,384]{0,1:T(8,128)S(1)}, f32[2048,384]{0,1:T(8,128)}, u32[]{:S(2)}) copy-start(f32[2048,384]{0,1:T(8,128)} %copy-done.7) | copy-start | bytes 9437188
  195.8 3.5 %copy-start.9 = (f32[2048,384]{0,1:T(8,128)S(1)}, f32[2048,384]{0,1:T(8,128)}, u32[]{:S(2)}) copy-start(f32[2048,384]{0,1:T(8,128)} %get-tuple-element.19) | copy-start | bytes 9437188
  195.8 8.8 %slice-start = ((s8[8388608]{0:T(1024)(128)(4,1)}), s8[4194304]{0:T(1024)(128)(4,1)S(1)}, s32[]{:S(2)}) async-start(s8[8388608]{0:T(1024)(128)(4,1)} %bitcast.53), calls=%async_computation | async-start | bytes 8388608
  199.3 5.3 %slice-start.1 = ((s8[8388608]{0:T(1024)(128)(4,1)}), s8[4194304]{0:T(1024)(128)(4,1)S(1)}, s32[]{:S(2)}) async-start(s8[8388608]{0:T(1024)(128)(4,1)} %bitcast.53), calls=%async_computation.1 | async-start | bytes 8388608
  211.4 7.7 %copy-start.1 = (bf16[1,2048,384]{2,1,0:T(8,128)(2,1)S(1)}, bf16[1,2048,384]{2,1,0:T(8,128)(2,1)}, u32[]{:S(2)}) copy-start(bf16[1,2048,384]{2,1,0:T(8,128)(2,1)} %param.15) | copy-start | bytes 4718596

commit v2 on v1

--- a/solution.py
+++ b/solution.py
@@ -241,6 +241,75 @@
     )(part)
 
 
+def forward_kernel(
+    core_ref, x_ref, scale_ref, wg_ref, wu_ref, vg_ref, vu_ref,
+    keep_ref, give_ref, act_ref, slope_ref, silu_ref, mats, held, sems,
+):
+    hidden = act_ref.shape[1]
+
+    @pl.when(pl.program_id(0) == 0)
+    def _():
+        copies = [
+            pltpu.make_async_copy(ref, mats.at[:, pl.ds(i * hidden, hidden)], sems.at[i])
+            for i, ref in enumerate((wg_ref, wu_ref, vg_ref, vu_ref))
+        ]
+        for copy in copies:
+            copy.start()
+        for copy in copies:
+            copy.wait()
+
+    wide = product(x_ref[...], mats[...])
+    pre_gate, pre_up, d_gate, d_up = (
+        wide[:, i * hidden:(i + 1) * hidden] for i in range(4)
+    )
+    silu_g, slope_g = silu_parts(pre_gate)
+    scale = scale_ref[...]
+    act_wide = silu_g * pre_up
+    up_slope = slope_g * pre_up
+    shape = held.shape[:3] + (hidden,)
+    d_act = (up_slope * d_gate + silu_g * d_up).astype(jnp.bfloat16)
+    held[:, :, :, :hidden] = d_act.reshape(shape)
+    held[:, :, :, hidden:] = act_wide.astype(jnp.bfloat16).reshape(shape)
+    act_ref[...] = (scale * act_wide).astype(jnp.bfloat16)
+    slope_ref[...] = scale * up_slope
+    silu_ref[...] = scale * silu_g
+    core = core_ref[0]
+    keep_ref[...] = held[:, core]
+    give_ref[...] = held[:, 1 - core]
+
+
+def forward(core, x, scale, mats, groups, half_tok):
+    count, width = x.shape
+    hidden = mats[0].shape[1]
+    tile = 256
+    pair = tile // (2 * half_tok)
+    flat = lambda cols: pl.BlockSpec((tile, cols), lambda i, core: (i, 0))
+    part = pl.BlockSpec((pair, half_tok, 2 * hidden), lambda i, core: (i, 0, 0))
+    row = lambda kind: jax.ShapeDtypeStruct((count, hidden), kind)
+    piece = jax.ShapeDtypeStruct((groups, half_tok, 2 * hidden), jnp.bfloat16)
+    return pl.pallas_call(
+        forward_kernel,
+        out_shape=(piece, piece, row(jnp.bfloat16), row(jnp.float32), row(jnp.float32)),
+        grid_spec=pltpu.PrefetchScalarGridSpec(
+            num_scalar_prefetch=1,
+            grid=(count // tile,),
+            in_specs=[flat(width), flat(1)] + [ANY] * 4,
+            out_specs=(part, part, flat(hidden), flat(hidden), flat(hidden)),
+            scratch_shapes=[
+                pltpu.VMEM((width, 4 * hidden), jnp.bfloat16),
+                pltpu.VMEM((pair, 2, half_tok, 2 * hidden), jnp.bfloat16),
+                pltpu.SemaphoreType.DMA((4,)),
+            ],
+        ),
+        compiler_params=pltpu.CompilerParams(vmem_limit_bytes=28 * 1024 * 1024),
+        cost_estimate=pl.CostEstimate(
+            flops=8 * count * width * hidden,
+            bytes_accessed=2 * count * width + 8 * width * hidden + 20 * count * hidden,
+            transcendentals=count * hidden,
+        ),
+    )(core, x, scale, *mats)
+
+
 def body(tokens, expert_ids, gates, token_weight, w_gate, w_up, w_down, v_gate, v_up, v_down):
     tok_count, width = tokens.shape
     picks = expert_ids.shape[1]
@@ -267,19 +336,10 @@
     mats = jnp.concatenate([down_mat, vdown_mat, down_other, vdown_other], axis=0)
 
     x = x_parts.reshape(groups * tok_count, width)
-    pre_gate = product(x, w_gate[0])
-    pre_up = product(x, w_up[0])
-    d_gate = product(x, v_gate[0])
-    d_up = product(x, v_up[0])
-    silu_g, slope_g = silu_parts(pre_gate)
-    act_wide = silu_g * pre_up
-    act = act_wide.astype(jnp.bfloat16)
-    d_act = (slope_g * d_gate * pre_up + silu_g * d_up).astype(jnp.bfloat16)
-
-    hidden = act.shape[1]
-    both = jnp.concatenate([d_act, act], axis=1).reshape(groups, 2, half_tok, 2 * hidden)
-    keep = lax.dynamic_index_in_dim(both, core, 1, keepdims=False)
-    give = lax.dynamic_index_in_dim(both, 1 - core, 1, keepdims=False)
+    keep, give, act_scaled, up_slope, silu_scaled = forward(
+        core.reshape(1), x, scale_of, (w_gate[0], w_up[0], v_gate[0], v_up[0]), groups, half_tok
+    )
+    hidden = act_scaled.shape[1]
     got = lax.ppermute(give, "tensor", swap)
     left = jnp.concatenate([keep, got], axis=2).reshape(groups * half_tok, 4 * hidden)
     gate_half = lax.dynamic_index_in_dim(
@@ -292,12 +352,11 @@
     tangent = lax.dynamic_slice(
         dy, (me * tok_count, core * (width // 2)), (tok_count, width // 2)
     )
-    back = scale_of * lax.dot_general(
+    back = lax.dot_general(
         dy, w_down[0], (((1,), (1,)), ((), ())), preferred_element_type=jnp.float32
     )
-    grad_gate = (back * pre_up * slope_g).astype(jnp.bfloat16)
-    grad_up = (back * silu_g).astype(jnp.bfloat16)
-    act_scaled = (scale_of * act_wide).astype(jnp.bfloat16)
+    grad_gate = (back * up_slope).astype(jnp.bfloat16)
+    grad_up = (back * silu_scaled).astype(jnp.bfloat16)
     factor = 1.0 / (tok_count * picks) ** 0.5
     return (
         (factor * contract_rows(x, grad_gate))[None],

time: 219 us -> 221 us (level)
  matrix products: 57.6 us -> 33 us
  Pallas kernels: 141 us -> 158 us
  local copies, waits for them, and re-layouts: 12.2 us -> 20.2 us
  waiting for transfers between devices: 3.25 us -> 5.78 us
    dot_general x5 -> x1, matrix products: 35.1 us -> 8.71 us  [product(): return jnp.dot(left, right, preferred_element_type=jnp.float32)]
    pallas_call x0 -> x1, Pallas kernels: none -> 16.5 us  [forward(): pl.pallas_call(forward_kernel, out_shape=(piece, piece, row(jnp.bfloat16)...]
    unnamed x24 -> x28, local copies, waits for them, and re-layouts: 4.31 us -> 17.8 us
    concatenate x1 -> x0, local copies, waits for them, and re-layouts: 4.72 us -> none  [body(): jnp.concatenate([d_act, act], axis=1)]
    dot_general x1, matrix products: 3.47 us -> 6.26 us  [body(): lax.dot_general(dy, w_down[0], (((1,), (1,)), ((), ())), preferred_elemen...]
    ppermute x1, waiting for transfers between devices: 0.01 us -> 2.25 us  [body(): vdown_other = lax.ppermute(vdown_send, 'tensor', swap)]
  transfers between devices with their start and end apart: 3 -> 3, of which waited for: 1 -> 3; matrix products, arithmetic and copies ran while one was open for 16% -> 1% of each run, Pallas kernels for 0% -> 0%
where the time goes in v2:
time: 221 us
  Pallas kernels  158 us (71%)
  matrix products  33 us (15%)
  local copies, waits for them, and re-layouts  20.2 us (9%)
  waiting for transfers between devices  5.78 us (3%)
  other arithmetic  3.16 us (1%)
    pallas_call x1, Pallas kernels, reduce_and_spread(): pl.pallas_call(functools.partial(reduce_kernel, depth), out_shape=jax.Sha...  89.9 us
    pallas_call x1, Pallas kernels, gather_tokens(): pl.pallas_call(functools.partial(gather_kernel, depth), out_shape=(jax.Sh...  51.3 us
    dot_general x3, matrix products, contract_rows(): lax.dot_general(left, right, (((0,), (0,)), ((), ())), preferred_element_...  18 us
    unnamed x28, local copies, waits for them, and re-layouts  17.8 us
    pallas_call x1, Pallas kernels, forward(): pl.pallas_call(forward_kernel, out_shape=(piece, piece, row(jnp.bfloat16)...  16.5 us
    dot_general x1, matrix products, product(): return jnp.dot(left, right, preferred_element_type=jnp.float32)  8.71 us
    dot_general x1, matrix products, body(): lax.dot_general(dy, w_down[0], (((1,), (1,)), ((), ())), preferred_elemen...  6.26 us
  transfers between devices with their start and end apart: 3, of which 3 were waited for; matrix products, arithmetic and copies ran while one was open for 1% of the time, Pallas kernels for 0%

profile of v2, /device:TPU:27, one launch (start us, length us, event | category | flops | bytes accessed | tf_op | source)
XLA Modules:
  0.0 221.1 jit_solution(16221457415813673408)
XLA Ops:
  0.6 0.1 pad.8.clone
  0.7 0.7 select_reduce_fusion
  1.4 0.7 maximum_maximum_fusion.table_ref
  2.2 0.0 copy-start.1
  2.2 1.0 copy-done.1
  3.2 51.3 %shard_map.129 = (bf16[16,2,64,2048]{3,2,1,0:T(8,128)(2,1)S(1)}, f32[16,24,128]{2,1,0:T(8,128)S(1)}) custom-call(bf16[2,64,2048]{2,1,0:T(8,128)(2,1)S(1)} %bitcast.34, f32[24,128]{1,0:T(8,128)S(1)} %maximum_maximum_fusion.table_ref), custom_call_target="tpu_custom_call" | custom-call | tf_op jit(solution)/shard_map/pallas_call | solution.py:206
  54.5 0.0 copy-start.2
  54.6 3.2 %copy-done.2 = bf16[16,2,64,2048]{3,2,1,0:T(8,128)(2,1)} copy-done((bf16[16,2,64,2048]{3,2,1,0:T(8,128)(2,1)}, bf16[16,2,64,2048]{3,2,1,0:T(8,128)(2,1)S(1)}, u32[]{:S(2)}) %copy-start.2) | copy-done | bytes 8388632
  57.8 1.3 copy.19.scale_ref
  59.2 0.0 copy-start
  59.2 1.2 copy-done
  60.4 0.0 copy-start.3
  60.4 3.4 %copy-done.3 = bf16[16,2,64,2048]{3,2,1,0:T(8,128)(2,1)S(1)} copy-done((bf16[16,2,64,2048]{3,2,1,0:T(8,128)(2,1)S(1)}, bf16[16,2,64,2048]{3,2,1,0:T(8,128)(2,1)}, u32[]{:S(2)}) %copy-start.3) | copy-done | bytes 8388632
  63.8 0.0 copy-start.4
  63.8 1.4 copy-done.4
  65.2 0.0 copy-start.5
  65.2 1.4 copy-done.5
  66.6 0.0 copy-start.6
  66.6 1.4 copy-done.6
  68.0 1.4 copy-done.7
  69.4 16.5 %shard_map.130 = (bf16[16,64,768]{2,1,0:T(8,128)(2,1)S(1)}, bf16[16,64,768]{2,1,0:T(8,128)(2,1)}, bf16[2048,384]{1,0:T(8,128)(2,1)S(1)}, f32[2048,384]{1,0:T(8,128)S(1)}, f32[2048,384]{1,0:T(8,128)S(1)}) custom-call(s32[1]{0:T(128)} %bitcast.6.core_ref, bf16[2048,2048]{1,0:T(8,128)(2,1)S(1)} %bitcast.35, f32[2048,1]{1,0:T(8,128)S(1)} %copy-done, ...), custom_call_target="tpu_custom_call" | custom-call | flops 12884901888 | bytes 30408704 | tf_op jit(solution)/shard_map/pallas_call | solution.py:290
  85.9 0.0 copy-start.8
  85.9 1.7 copy-done.8
  87.5 1.7 copy-done.10
  89.2 0.1 collective-permute-start
  89.3 0.4 collective-permute-start.1
  89.7 0.1 collective-permute-start.2
  89.8 0.1 reshape_reshape.3
  89.9 0.1 mul.43
  90.0 3.0 %collective-permute-done = bf16[16,64,768]{2,1,0:T(8,128)(2,1)} collective-permute-done((bf16[16,64,768]{2,1,0:T(8,128)(2,1)}, bf16[16,64,768]{2,1,0:T(8,128)(2,1)}, u32[]{:S(2)}, u32[]{:S(2)}) %collective-permute-start) | collective-permute-done | bytes 1572896 | tf_op jit(solution)/shard_map/ppermute | solution.py:343
  92.9 1.7 pad_maximum_fusion
  94.6 0.6 collective-permute-done.1
  95.2 2.2 %collective-permute-done.2 = bf16[384,2048]{1,0:T(8,128)(2,1)} collective-permute-done((bf16[384,2048]{1,0:T(8,128)(2,1)}, bf16[384,2048]{1,0:T(8,128)(2,1)}, u32[]{:S(2)}, u32[]{:S(2)}) %collective-permute-start.2) | collective-permute-done | bytes 1572896 | tf_op jit(solution)/shard_map/ppermute | solution.py:335
  97.4 8.7 %multiply_convert_fusion = bf16[1024,2048]{1,0:T(8,128)(2,1)S(1)} fusion(f32[1024]{0:T(1024)S(1)} %mul.43, bf16[1024,1536]{1,0:T(8,128)(2,1)S(1)} %bitcast.44, bf16[384,2048]{1,0:T(8,128)(2,1)} %collective-permute-done.2, bf16[384,2048]{1,0:T(8,128)(2,1)} %collective-permute-done.1, bf16[384,2048]{1,0:T(8,128)(2,1)} %bitcast.4, bf16[384,2048]{1,0:T(8,128)(2,1)} %bitcast.3), kind=kOutput, calls=%fused_computation | convolution fusion | flops 6471811072 | bytes 13635584 | tf_op jit(solution)/shard_map/dot_general | solution.py:16
  106.2 0.0 slice-start
  106.2 89.9 %shard_map.131 = bf16[16,2,64,2048]{3,2,1,0:T(8,128)(2,1)S(1)} custom-call(bf16[16,64,2048]{2,1,0:T(8,128)(2,1)S(1)} %bitcast.33), custom_call_target="tpu_custom_call" | custom-call | tf_op jit(solution)/shard_map/pallas_call | solution.py:227
  196.0 0.0 slice-start.1
  196.1 6.3 %fusion.11 = f32[2048,384]{1,0:T(8,128)S(1)} fusion(bf16[2048,2048]{1,0:T(8,128)(2,1)S(1)} %bitcast.30, bf16[1,384,2048]{2,1,0:T(8,128)(2,1)} %param.16), kind=kOutput, calls=%fused_computation.22 | convolution fusion | flops 3221225472 | bytes 13107200 | tf_op jit(solution)/shard_map/dot_general | solution.py:355
  202.3 0.0 copy-start.11
  202.3 5.3 %multiply_bitcast_fusion = f32[1,384,2048]{2,1,0:T(8,128)} fusion(bf16[2048,384]{1,0:T(8,128)(2,1)S(1)} %get-tuple-element.23, bf16[2048,2048]{1,0:T(8,128)(2,1)S(1)} %bitcast.31), kind=kOutput, calls=%fused_computation.10 | convolution fusion | flops 3222011904 | bytes 13107200 | tf_op jit(solution)/shard_map/dot_general | solution.py:20
  207.6 0.0 slice-done
  207.6 0.0 slice-done.1
  207.6 0.0 copy-done.11
  207.6 0.0 copy-start.9
  207.6 6.2 %multiply_bitcast_fusion.1 = f32[1,2048,384]{2,1,0:T(8,128)} fusion(bf16[2048,2048]{1,0:T(8,128)(2,1)S(1)} %bitcast.38, f32[2048,384]{1,0:T(8,128)S(1)} %fusion.11, f32[2048,384]{1,0:T(8,128)S(1)} %copy-done.11), kind=kOutput, calls=%fused_computation.11 | convolution fusion | flops 3223584768 | bytes 17825792 | tf_op jit(solution)/shard_map/dot_general | solution.py:20
  213.9 0.0 copy-done.9
  213.9 6.5 %multiply_bitcast_fusion.2 = f32[1,2048,384]{2,1,0:T(8,128)} fusion(bf16[2048,2048]{1,0:T(8,128)(2,1)S(1)} %bitcast.39, f32[2048,384]{1,0:T(8,128)S(1)} %fusion.11, f32[2048,384]{1,0:T(8,128)S(1)} %copy-done.9), kind=kOutput, calls=%fused_computation.13 | convolution fusion | flops 3223584768 | bytes 17825792 | tf_op jit(solution)/shard_map/dot_general | solution.py:20
  220.3 0.7 dynamic_slice.13
  (6 shorter events, 0.1 us)
Async XLA Ops:
  2.2 1.0 copy-start.1
  54.5 3.2 %copy-start.2 = (bf16[16,2,64,2048]{3,2,1,0:T(8,128)(2,1)}, bf16[16,2,64,2048]{3,2,1,0:T(8,128)(2,1)S(1)}, u32[]{:S(2)}) copy-start(bf16[16,2,64,2048]{3,2,1,0:T(8,128)(2,1)S(1)} %get-tuple-element.15) | copy-start | bytes 25165828
  59.2 1.2 copy-start
  60.4 3.4 %copy-start.3 = (bf16[16,2,64,2048]{3,2,1,0:T(8,128)(2,1)S(1)}, bf16[16,2,64,2048]{3,2,1,0:T(8,128)(2,1)}, u32[]{:S(2)}) copy-start(bf16[16,2,64,2048]{3,2,1,0:T(8,128)(2,1)} %copy-done.2) | copy-start | bytes 25165828
  63.8 1.4 copy-start.4
  65.2 1.4 copy-start.5
  66.6 1.4 copy-start.6
  68.0 1.4 copy-start.7
  85.9 1.7 copy-start.8
  87.5 1.7 copy-start.10
  89.2 3.8 %collective-permute-start = (bf16[16,64,768]{2,1,0:T(8,128)(2,1)}, bf16[16,64,768]{2,1,0:T(8,128)(2,1)}, u32[]{:S(2)}, u32[]{:S(2)}) collective-permute-start(bf16[16,64,768]{2,1,0:T(8,128)(2,1)} %get-tuple-element.18), channel_id=1, source_target_pairs={{0,1},{1,0},{2,3},{3,2},{4,5},{5,4},{6,7},{7,6},{8,9},{9,8},{10,11... | collective-permute-start | bytes 4718600 | tf_op jit(solution)/shard_map/ppermute | solution.py:343
  89.3 5.9 %collective-permute-start.1 = (bf16[384,2048]{1,0:T(8,128)(2,1)}, bf16[384,2048]{1,0:T(8,128)(2,1)}, u32[]{:S(2)}, u32[]{:S(2)}) collective-permute-start(bf16[384,2048]{1,0:T(8,128)(2,1)} %bitcast.3), channel_id=1, source_target_pairs={{0,1},{1,0},{2,3},{3,2},{4,5},{5,4},{6,7},{7,6},{8,9},{9,8},{10,11... | collective-permute-start | bytes 4718600 | tf_op jit(solution)/shard_map/ppermute | solution.py:334
  89.7 7.7 %collective-permute-start.2 = (bf16[384,2048]{1,0:T(8,128)(2,1)}, bf16[384,2048]{1,0:T(8,128)(2,1)}, u32[]{:S(2)}, u32[]{:S(2)}) collective-permute-start(bf16[384,2048]{1,0:T(8,128)(2,1)} %bitcast.4), channel_id=1, source_target_pairs={{0,1},{1,0},{2,3},{3,2},{4,5},{5,4},{6,7},{7,6},{8,9},{9,8},{10,11... | collective-permute-start | bytes 4718600 | tf_op jit(solution)/shard_map/ppermute | solution.py:335
  106.2 101.4 %slice-start = ((s8[8388608]{0:T(1024)(128)(4,1)}), s8[4194304]{0:T(1024)(128)(4,1)S(1)}, s32[]{:S(2)}) async-start(s8[8388608]{0:T(1024)(128)(4,1)} %bitcast.36), calls=%async_computation | async-start | bytes 8388608
  196.0 11.6 %slice-start.1 = ((s8[8388608]{0:T(1024)(128)(4,1)}), s8[4194304]{0:T(1024)(128)(4,1)S(1)}, s32[]{:S(2)}) async-start(s8[8388608]{0:T(1024)(128)(4,1)} %bitcast.36), calls=%async_computation.1 | async-start | bytes 8388608
  202.3 5.3 %copy-start.11 = (f32[2048,384]{1,0:T(8,128)S(1)}, f32[2048,384]{1,0:T(8,128)}, u32[]{:S(2)}) copy-start(f32[2048,384]{1,0:T(8,128)} %copy-done.10) | copy-start | bytes 9437188
  207.6 6.2 %copy-start.9 = (f32[2048,384]{1,0:T(8,128)S(1)}, f32[2048,384]{1,0:T(8,128)}, u32[]{:S(2)}) copy-start(f32[2048,384]{1,0:T(8,128)} %copy-done.8) | copy-start | bytes 9437188

commit v3 on v2

--- a/solution.py
+++ b/solution.py
@@ -213,7 +213,10 @@
         out_specs=(ANY, ANY),
         scratch_shapes=[dma((12, depth)), dma((12, depth)), dma((1,))],
         compiler_params=pltpu.CompilerParams(
-            collective_id=0, has_side_effects=True, vmem_limit_bytes=2 * 1024 * 1024
+            collective_id=0, has_side_effects=True, vmem_limit_bytes=60 * 1024 * 1024
+        ),
+        cost_estimate=pl.CostEstimate(
+            flops=0, bytes_accessed=8 * groups * count * width, transcendentals=0
         ),
     )(tokens.reshape(2, half, width), table)
 
@@ -301,7 +304,7 @@
                 pltpu.SemaphoreType.DMA((4,)),
             ],
         ),
-        compiler_params=pltpu.CompilerParams(vmem_limit_bytes=28 * 1024 * 1024),
+        compiler_params=pltpu.CompilerParams(vmem_limit_bytes=60 * 1024 * 1024),
         cost_estimate=pl.CostEstimate(
             flops=8 * count * width * hidden,
             bytes_accessed=2 * count * width + 8 * width * hidden + 20 * count * hidden,
@@ -329,10 +332,12 @@
     gate_of = lax.dynamic_index_in_dim(tables, me, 1, keepdims=False).reshape(-1, 1)
     scale_of = gate_of * tables[:, groups].reshape(-1, 1)
     down_mat, vdown_mat = w_down[0], v_down[0]
-    x_parts, down_send, vdown_send = lax.optimization_barrier((x_parts, down_mat, vdown_mat))
     swap = [(0, 1), (1, 0)]
-    down_other = lax.ppermute(down_send, "tensor", swap)
-    vdown_other = lax.ppermute(vdown_send, "tensor", swap)
+    down_other = lax.ppermute(down_mat, "tensor", swap)
+    vdown_other = lax.ppermute(vdown_mat, "tensor", swap)
+    x_parts, down_other, vdown_other = lax.optimization_barrier(
+        (x_parts, down_other, vdown_other)
+    )
     mats = jnp.concatenate([down_mat, vdown_mat, down_other, vdown_other], axis=0)
 
     x = x_parts.reshape(groups * tok_count, width)

time: 221 us -> 208 us (0.941)
  local copies, waits for them, and re-layouts: 20.2 us -> 3.36 us
  Pallas kernels: 158 us -> 165 us
  matrix products: 33 us -> 29.8 us
  waiting for transfers between devices: 5.78 us -> 3.35 us
    unnamed x28 -> x18, local copies, waits for them, and re-layouts: 17.8 us -> 1.03 us
    pallas_call x1, Pallas kernels: 16.5 us -> 20.7 us  [forward(): pl.pallas_call(forward_kernel, out_shape=(piece, piece, row(jnp.bfloat16)...]
    ppermute x2, waiting for transfers between devices: 2.81 us -> 0.01 us  [the longest x1 0.01 us: body(): down_other = lax.ppermute(down_mat, 'tensor', swap)]
    pallas_call x1, Pallas kernels: 51.3 us -> 54 us  [gather_tokens(): pl.pallas_call(functools.partial(gather_kernel, depth), out_shape=(jax.Sh...]
  transfers between devices with their start and end apart: 3 -> 3, of which waited for: 3 -> 1; matrix products, arithmetic and copies ran while one was open for 1% -> 2% of each run, Pallas kernels for 0% -> 26%
where the time goes in v3:
time: 208 us
  Pallas kernels  165 us (79%)
  matrix products  29.8 us (14%)
  other arithmetic  4.77 us (2%)
  local copies, waits for them, and re-layouts  3.36 us (2%)
  waiting for transfers between devices  3.35 us (2%)
    pallas_call x1, Pallas kernels, reduce_and_spread(): pl.pallas_call(functools.partial(reduce_kernel, depth), out_shape=jax.Sha...  89.8 us
    pallas_call x1, Pallas kernels, gather_tokens(): pl.pallas_call(functools.partial(gather_kernel, depth), out_shape=(jax.Sh...  54 us
    pallas_call x1, Pallas kernels, forward(): pl.pallas_call(forward_kernel, out_shape=(piece, piece, row(jnp.bfloat16)...  20.7 us
    dot_general x3, matrix products, contract_rows(): lax.dot_general(left, right, (((0,), (0,)), ((), ())), preferred_element_...  18.4 us
    dot_general x1, matrix products, product(): return jnp.dot(left, right, preferred_element_type=jnp.float32)  6.87 us
    dot_general x1, matrix products, body(): lax.dot_general(dy, w_down[0], (((1,), (1,)), ((), ())), preferred_elemen...  4.55 us
  transfers between devices with their start and end apart: 3, of which 1 were waited for; matrix products, arithmetic and copies ran while one was open for 2% of the time, Pallas kernels for 26%

profile of v3, /device:TPU:27, one launch (start us, length us, event | category | flops | bytes accessed | tf_op | source)
XLA Modules:
  0.0 207.5 jit_solution(6635588669809974123)
XLA Ops:
  0.6 0.7 collective-permute-start.1
  1.4 0.1 collective-permute-start
  1.5 0.1 pad.8.clone
  1.5 0.7 select_reduce_fusion
  2.2 1.3 maximum_maximum_fusion.table_ref
  3.6 54.0 %shard_map.129 = (bf16[16,2,64,2048]{3,2,1,0:T(8,128)(2,1)}, f32[16,24,128]{2,1,0:T(8,128)}) custom-call(bf16[2,64,2048]{2,1,0:T(8,128)(2,1)} %bitcast.35, f32[24,128]{1,0:T(8,128)} %maximum_maximum_fusion.table_ref), custom_call_target="tpu_custom_call" | custom-call | bytes 33554432 | tf_op jit(solution)/shard_map/pallas_call | solution.py:206
  57.6 0.9 multiply_bitcast_fusion.3
  58.5 1.3 copy.19.scale_ref
  59.8 0.0 collective-permute-done.1
  59.8 0.0 collective-permute-done
  59.8 0.0 copy-start.3
  59.8 20.7 %shard_map.130 = (bf16[16,64,768]{2,1,0:T(8,128)(2,1)}, bf16[16,64,768]{2,1,0:T(8,128)(2,1)}, bf16[2048,384]{1,0:T(8,128)(2,1)}, f32[2048,384]{1,0:T(8,128)}, f32[2048,384]{1,0:T(8,128)}) custom-call(s32[1]{0:T(128)} %bitcast.6.core_ref, bf16[2048,2048]{1,0:T(8,128)(2,1)} %bitcast.38, f32[2048,1]{1,0:T(8,128)} %copy.19.scale_ref, ...), custom_call_target="tpu_custom_call" | custom-call | flops 12884901888 | bytes 30408704 | tf_op jit(solution)/shard_map/pallas_call | solution.py:293
  80.6 0.0 copy-done.3
  80.6 0.2 collective-permute-start.2
  80.7 0.1 reshape_reshape.3
  80.8 0.1 mul.43
  80.9 3.3 %collective-permute-done.2 = bf16[16,64,768]{2,1,0:T(8,128)(2,1)S(1)} collective-permute-done((bf16[16,64,768]{2,1,0:T(8,128)(2,1)}, bf16[16,64,768]{2,1,0:T(8,128)(2,1)S(1)}, u32[]{:S(2)}, u32[]{:S(2)}) %collective-permute-start.2) | collective-permute-done | bytes 1572896 | tf_op jit(solution)/shard_map/ppermute | solution.py:348
  84.3 0.0 copy-start.1
  84.3 0.0 copy-start.2
  84.3 0.0 copy-start.4
  84.3 1.8 pad_maximum_fusion
  86.1 0.1 copy-done.1
  86.1 0.5 copy-done.2
  86.6 0.5 copy-done.4
  87.1 6.9 %multiply_convert_fusion = bf16[1024,2048]{1,0:T(8,128)(2,1)S(1)} fusion(f32[1024]{0:T(1024)S(1)} %mul.43, bf16[1024,1536]{1,0:T(8,128)(2,1)S(1)} %bitcast.34, bf16[384,2048]{1,0:T(8,128)(2,1)S(1)} %collective-permute-done.1, bf16[384,2048]{1,0:T(8,128)(2,1)S(1)} %copy-done.4, bf16[384,2048]{1,0:T(8,128)(2,1)S(1)} %bitcast.48, bf16[384,2048]{1,0:T(8,128)(2,1)S(1)} %bitcast.50), kind=kOutput, calls=%fused_computation | convolution fusion | flops 6471811072 | bytes 13635584 | tf_op jit(solution)/shard_map/dot_general | solution.py:16
  94.0 0.0 slice-start
  94.0 89.8 %shard_map.131 = bf16[16,2,64,2048]{3,2,1,0:T(8,128)(2,1)S(1)} custom-call(bf16[16,64,2048]{2,1,0:T(8,128)(2,1)S(1)} %bitcast.33), custom_call_target="tpu_custom_call" | custom-call | tf_op jit(solution)/shard_map/pallas_call | solution.py:230
  183.8 0.0 copy-start
  183.8 0.0 slice-start.1
  183.8 4.5 %fusion.11 = f32[2048,384]{1,0:T(8,128)S(1)} fusion(bf16[2048,2048]{1,0:T(8,128)(2,1)S(1)} %bitcast.30, bf16[1,384,2048]{2,1,0:T(8,128)(2,1)S(1)} %copy-done.2), kind=kOutput, calls=%fused_computation.22 | convolution fusion | flops 3221225472 | bytes 13107200 | tf_op jit(solution)/shard_map/dot_general | solution.py:360
  188.4 0.0 copy-done
  188.4 0.0 copy-start.6
  188.4 5.3 %multiply_bitcast_fusion = f32[1,384,2048]{2,1,0:T(8,128)} fusion(bf16[2048,384]{1,0:T(8,128)(2,1)S(1)} %copy-done, bf16[2048,2048]{1,0:T(8,128)(2,1)S(1)} %bitcast.31), kind=kOutput, calls=%fused_computation.10 | convolution fusion | flops 3222011904 | bytes 13107200 | tf_op jit(solution)/shard_map/dot_general | solution.py:20
  193.7 0.0 slice-done
  193.7 0.0 slice-done.1
  193.7 0.0 copy-done.6
  193.7 0.0 copy-start.5
  193.7 6.4 %multiply_bitcast_fusion.1 = f32[1,2048,384]{2,1,0:T(8,128)} fusion(bf16[2048,2048]{1,0:T(8,128)(2,1)S(1)} %bitcast.41, f32[2048,384]{1,0:T(8,128)S(1)} %fusion.11, f32[2048,384]{1,0:T(8,128)S(1)} %copy-done.6), kind=kOutput, calls=%fused_computation.11 | convolution fusion | flops 3223584768 | bytes 17825792 | tf_op jit(solution)/shard_map/dot_general | solution.py:20
  200.1 0.0 copy-done.5
  200.1 6.7 %multiply_bitcast_fusion.2 = f32[1,2048,384]{2,1,0:T(8,128)} fusion(bf16[2048,2048]{1,0:T(8,128)(2,1)S(1)} %bitcast.42, f32[2048,384]{1,0:T(8,128)S(1)} %fusion.11, f32[2048,384]{1,0:T(8,128)S(1)} %copy-done.5), kind=kOutput, calls=%fused_computation.13 | convolution fusion | flops 3223584768 | bytes 17825792 | tf_op jit(solution)/shard_map/dot_general | solution.py:20
  206.8 0.7 dynamic_slice.13
  (3 shorter events, 0.0 us)
Async XLA Ops:
  0.6 59.2 %collective-permute-start.1 = (bf16[384,2048]{1,0:T(8,128)(2,1)}, bf16[384,2048]{1,0:T(8,128)(2,1)S(1)}, u32[]{:S(2)}, u32[]{:S(2)}) collective-permute-start(bf16[384,2048]{1,0:T(8,128)(2,1)} %bitcast.47), channel_id=1, source_target_pairs={{0,1},{1,0},{2,3},{3,2},{4,5},{5,4},{6,7},{7,6},{8,9},{9,8},{10,11... | collective-permute-start | bytes 4718600 | tf_op jit(solution)/shard_map/ppermute | solution.py:337
  1.4 58.4 %collective-permute-start = (bf16[384,2048]{1,0:T(8,128)(2,1)}, bf16[384,2048]{1,0:T(8,128)(2,1)S(1)}, u32[]{:S(2)}, u32[]{:S(2)}) collective-permute-start(bf16[384,2048]{1,0:T(8,128)(2,1)} %bitcast.49), channel_id=1, source_target_pairs={{0,1},{1,0},{2,3},{3,2},{4,5},{5,4},{6,7},{7,6},{8,9},{9,8},{10,11... | collective-permute-start | bytes 4718600 | tf_op jit(solution)/shard_map/ppermute | solution.py:336
  59.8 20.7 %copy-start.3 = (bf16[384,2048]{1,0:T(8,128)(2,1)}, bf16[384,2048]{1,0:T(8,128)(2,1)S(1)}, u32[]{:S(2)}) copy-start(bf16[384,2048]{1,0:T(8,128)(2,1)S(1)} %collective-permute-done) | copy-start | bytes 4718596
  80.6 3.7 %collective-permute-start.2 = (bf16[16,64,768]{2,1,0:T(8,128)(2,1)}, bf16[16,64,768]{2,1,0:T(8,128)(2,1)S(1)}, u32[]{:S(2)}, u32[]{:S(2)}) collective-permute-start(bf16[16,64,768]{2,1,0:T(8,128)(2,1)} %get-tuple-element.18), channel_id=1, source_target_pairs={{0,1},{1,0},{2,3},{3,2},{4,5},{5,4},{6,7},{7,6},{8,9},{9,8},{10,11... | collective-permute-start | bytes 4718600 | tf_op jit(solution)/shard_map/ppermute | solution.py:348
  84.3 1.9 copy-start.1
  84.3 2.4 %copy-start.2 = (bf16[1,384,2048]{2,1,0:T(8,128)(2,1)S(1)}, bf16[1,384,2048]{2,1,0:T(8,128)(2,1)}, u32[]{:S(2)}) copy-start(bf16[1,384,2048]{2,1,0:T(8,128)(2,1)} %param.16) | copy-start | bytes 4718596
  84.3 2.8 %copy-start.4 = (bf16[384,2048]{1,0:T(8,128)(2,1)S(1)}, bf16[384,2048]{1,0:T(8,128)(2,1)}, u32[]{:S(2)}) copy-start(bf16[384,2048]{1,0:T(8,128)(2,1)} %copy-done.3) | copy-start | bytes 4718596
  94.0 99.7 %slice-start = ((s8[8388608]{0:T(1024)(128)(4,1)}), s8[4194304]{0:T(1024)(128)(4,1)S(1)}, s32[]{:S(2)}) async-start(s8[8388608]{0:T(1024)(128)(4,1)} %bitcast.39), calls=%async_computation | async-start | bytes 8388608
  183.8 4.6 %copy-start = (bf16[2048,384]{1,0:T(8,128)(2,1)S(1)}, bf16[2048,384]{1,0:T(8,128)(2,1)}, u32[]{:S(2)}) copy-start(bf16[2048,384]{1,0:T(8,128)(2,1)} %get-tuple-element.23) | copy-start | bytes 4718596
  183.8 9.9 %slice-start.1 = ((s8[8388608]{0:T(1024)(128)(4,1)}), s8[4194304]{0:T(1024)(128)(4,1)S(1)}, s32[]{:S(2)}) async-start(s8[8388608]{0:T(1024)(128)(4,1)} %bitcast.39), calls=%async_computation.1 | async-start | bytes 8388608
  188.4 5.3 %copy-start.6 = (f32[2048,384]{1,0:T(8,128)S(1)}, f32[2048,384]{1,0:T(8,128)}, u32[]{:S(2)}) copy-start(f32[2048,384]{1,0:T(8,128)} %get-tuple-element.22) | copy-start | bytes 9437188
  193.7 6.4 %copy-start.5 = (f32[2048,384]{1,0:T(8,128)S(1)}, f32[2048,384]{1,0:T(8,128)}, u32[]{:S(2)}) copy-start(f32[2048,384]{1,0:T(8,128)} %get-tuple-element.21) | copy-start | bytes 9437188
